TPU v7x, 128 devices: a whole 4x4x4 slice. The times are simulated.
128 devices in a mesh: gx: 8 (over y, core), gy: 16 (over z, x).
Axes of the slice: x: 4, y: 4, z: 4, core: 2. Of those that a mesh axis runs over, the one named last changes fastest.
Arguments:
- former_place_tile: int32 [32768], P(('gx', 'gy')), may hold values from -1 to 16383, as said below
- former_warmth: float32 [32768, 4096], P(('gx', 'gy')), may hold values from -6 to 6
- forcing_term: bfloat16 [32768, 4096], P(('gx', 'gy')), may hold values from -6 to 6
- diffusivity_map: bfloat16 [32768, 4096], P(('gx', 'gy')), may hold values from 0.5 to 8
- subdivision_depth: int32 [16384], P(('gx', 'gy')), may hold values from 0 to 2
- adjoining_tile: int32 [6, 16384], P(None, ('gx', 'gy')), may hold values from -1 to 16383, as said below
- adjoining_side: int32 [6, 16384], P(None, ('gx', 'gy')), may hold values from 0 to 5, as said below
- adjoining_rotation: int32 [6, 16384], P(None, ('gx', 'gy')), may hold values from 0 to 7, as said below
Outputs:
- new_temperature: float32 [16384, 4096], P(('gx', 'gy'))
Inputs may be any that keep to these rules, and one draw needn't show every extreme that they name: `former_place_tile`: each block id 0 to 16383 stands in exactly one slot and every other slot holds -1. Block b belongs to owner b // 128, the device at that position along gx+gy. The 256 slots of one device hold at most 2 blocks of any one owner, and for every owner some device holds exactly 2 of its blocks. -1 marks a face without a link. Links are mutual: if adjoining_tile[f, b] = c and adjoining_side[f, b] = g then adjoining_tile[g, c] = b and adjoining_side[g, c] = f. The linked faces of a block name different blocks. A linked block belongs to the same owner or to the owner one step away along gx or along gy with the same index on the other axis; a block has at most one linked face toward any other owner, and every two owners adjacent in this way share exactly 32 links. `adjoining_side`: 0 where adjoining_tile is -1. `adjoining_rotation`: the two sides of a link carry inverse turns: where one side has o, the other has o if o < 4, else 4 + 2 (o % 2) + (o // 2) % 2. 0 where adjoining_tile is -1.
All inputs are finite; a program needn't handle non-finite values.
Results may differ from a plain program's by a relative error of at most 0.00045.
Values may be sent and summed in bfloat16 or wider, within the bound.
A program may use at most 192 MiB of HBM per device.

v0:
```python
import functools

import jax
import jax.numpy as jnp
from jax import lax
from jax.experimental import pallas as pl
from jax.experimental.pallas import tpu as pltpu
from jax.sharding import PartitionSpec as P

B = 16
PLANE = B * B
CELLS = B * B * B
SWEEPS = 3
MASS_TERM = 4.0
LOWER_BOUND = 0.25
UPPER_BOUND = 2.0
CHUNK = 128
PAD = PLANE
LEVELS = 32767.0
F32 = jnp.float32
BF16 = jnp.bfloat16
I32 = jnp.int32
MESH = pl.DeviceIdType.MESH


def dot(a, b):
    return jnp.dot(a, b, preferred_element_type=F32)


def plane_rows(ref, base, face):
    if face == 0:
        return ref[pl.ds(base, PLANE), :]
    if face == 1:
        return ref[pl.ds(base + 15 * PLANE, PLANE), :]
    if face in (2, 3):
        first = base + (0 if face == 2 else PLANE - B)
        return jnp.concatenate([ref[pl.ds(first + PLANE * u, B), :] for u in range(B)], axis=0)
    return ref[pl.ds(base + (0 if face == 4 else B - 1), PLANE, stride=B), :]


def crossed_groups(ref, base, face):
    if face < 2:
        first, step, stride = base + 15 * PLANE * face, 1, B
    elif face < 4:
        first, step, stride = base + (PLANE - B) * (face - 2), 1, PLANE
    else:
        first, step, stride = base + (B - 1) * (face - 4), B, PLANE
    return [ref[pl.ds(first + step * v, B, stride=stride), :] for v in range(B)]


def face_update(ref, base, face, added):
    if face < 2:
        at = pl.ds(base + 15 * PLANE * face, PLANE)
        ref[at, :] = ref[at, :] + added
    elif face < 4:
        first = base + (PLANE - B) * (face - 2)
        for u in range(B):
            at = pl.ds(first + PLANE * u, B)
            ref[at, :] = ref[at, :] + added[u * B : (u + 1) * B]
    else:
        at = pl.ds(base + (B - 1) * (face - 4), PLANE, stride=B)
        ref[at, :] = ref[at, :] + added


def harmonic(p, q):
    return 2.0 * p * q / (p + q)


def kernel(
    devices,
    minor,
    place_ref,
    depth_ref,
    tile_ref,
    side_ref,
    turn_ref,
    warm_hbm,
    heat_hbm,
    kappa_hbm,
    out_ref,
    warm_in,
    heat_in,
    kappa_in,
    meta_out,
    meta_got,
    words_out,
    words_got,
    onehot,
    settle,
    conduct,
    link_i,
    link_j,
    link_k,
    right,
    inverse,
    field_a,
    field_b,
    change,
    gather,
    choose,
    turned,
    high,
    low,
    leaving,
    arriving,
    face_link,
    load_sem,
    meta_sems,
    send_sems,
    recv_sems,
    face_send,
    face_recv,
):
    major = devices // minor
    gx = lax.axis_index("gx")
    gy = lax.axis_index("gy")
    me = gx * minor + gy
    slots = place_ref.shape[1]
    lanes = 128
    barrier = pltpu.get_barrier_semaphore()

    def peer(t):
        p = lax.rem(me + t, devices)
        return p, (p // minor, lax.rem(p, minor))

    def greet(t, carry):
        pl.semaphore_signal(barrier, inc=1, device_id=peer(t)[1], device_id_type=MESH)
        return carry

    loads = [
        pltpu.make_async_copy(kappa_hbm, kappa_in, load_sem.at[0]),
        pltpu.make_async_copy(warm_hbm, warm_in, load_sem.at[1]),
        pltpu.make_async_copy(heat_hbm, heat_in, load_sem.at[2]),
    ]
    for copy in loads:
        copy.start()
    lax.fori_loop(1, devices, greet, 0)

    place_row = place_ref[...].astype(F32)
    row_id = lax.broadcasted_iota(I32, (slots, slots), 0)
    col_id = lax.broadcasted_iota(I32, (slots, slots), 1)
    place_wide = jnp.broadcast_to(place_row, (slots, slots))
    place_col = jnp.sum(jnp.where(row_id == col_id, place_wide, 0.0), axis=1, keepdims=True)
    owner_row = jnp.floor(place_wide * (1.0 / lanes))
    owner_col = jnp.floor(place_col * (1.0 / lanes))
    again = jnp.sum(
        jnp.where((owner_row == owner_col) & (row_id < col_id), 1.0, 0.0), axis=0, keepdims=True
    )
    row_at = jnp.where(place_row >= 0.0, again * devices + owner_row[:1], -1.0)
    onehot[...] = jnp.where(row_id.astype(F32) == row_at, 1.0, 0.0).astype(BF16)
    tag_col = jnp.where(place_col >= 0.0, place_col - owner_col * lanes + 1.0, 0.0)
    tags = dot(onehot[...], jnp.broadcast_to(tag_col, (slots, lanes)).astype(BF16))

    def put_words(field, t, words):
        for s in range(2):
            words_out[field, pl.ds(s * B + t, devices, stride=2 * B), :] = words[
                s * devices : (s + 1) * devices
            ]

    def send_field(field):
        def one(t, carry):
            p, where = peer(t)
            pltpu.make_async_remote_copy(
                words_out.at[field, pl.ds(pl.multiple_of(p * 2 * B, 2 * B), 2 * B)],
                words_got.at[field, pl.ds(pl.multiple_of(me * 2 * B, 2 * B), 2 * B)],
                send_sems.at[field],
                recv_sems.at[field],
                device_id=where,
                device_id_type=MESH,
            ).start()
            return carry

        lax.fori_loop(1, devices, one, 0)
        mine = pl.ds(pl.multiple_of(me * 2 * B, 2 * B), 2 * B)
        words_got[field, mine, :] = words_out[field, mine, :]

    loads[0].wait()

    def pack_kappa(t, carry):
        both = dot(onehot[...], kappa_in[:, pl.ds(pl.multiple_of(t * PLANE, PLANE), PLANE)])
        ints = (both * 256.0).astype(I32)
        put_words(0, t, ints[:, :lanes] + ints[:, lanes:] * 65536)
        return carry

    lax.fori_loop(0, B, pack_kappa, 0)
    pl.semaphore_wait(barrier, devices - 1)
    send_field(0)

    loads[1].wait()
    loads[2].wait()

    def scale_of(ref):
        def one(t, best):
            at = pl.ds(pl.multiple_of(t * lanes, lanes), lanes)
            return jnp.maximum(best, jnp.abs(ref[:, at].astype(F32)))

        best = lax.fori_loop(0, CELLS // lanes, one, jnp.zeros((slots, lanes), F32))
        largest = jnp.maximum(jnp.max(best, axis=1, keepdims=True) * 1.005, 1e-30)
        return dot(onehot[...], jnp.broadcast_to(largest, (slots, lanes)).astype(BF16))

    warm_scale = scale_of(warm_in)
    heat_scale = scale_of(heat_in)
    lane_id = lax.broadcasted_iota(I32, (devices, lanes), 1)
    meta = jnp.zeros((devices, lanes), F32)
    for n, part in enumerate((tags, warm_scale, heat_scale)):
        for s in range(2):
            meta = jnp.where(lane_id == 2 * n + s, part[s * devices : (s + 1) * devices], meta)
    meta_out[...] = meta.reshape(devices, 1, lanes)
    meta_got[pl.ds(me, 1)] = meta_out[pl.ds(me, 1)]

    def send_meta(t, carry):
        p, where = peer(t)
        pltpu.make_async_remote_copy(
            meta_out.at[p],
            meta_got.at[me],
            meta_sems.at[0],
            meta_sems.at[1],
            device_id=where,
            device_id_type=MESH,
        ).start()
        return carry

    lax.fori_loop(1, devices, send_meta, 0)

    def factor(scale):
        return jnp.where(scale > 0.0, LEVELS / jnp.maximum(scale, 1e-31), 0.0)

    warm_factor = factor(warm_scale)
    heat_factor = factor(heat_scale)

    def words_of(both, scale):
        ints = [jnp.round(both[:, c * lanes : (c + 1) * lanes] * scale).astype(I32) for c in (0, 1)]
        return ints[0] + ints[1] * 65536

    def pack_warm(t, carry):
        value = warm_in[:, pl.ds(pl.multiple_of(t * PLANE, PLANE), PLANE)]
        top = value.astype(BF16)
        rest = (value - top.astype(F32)).astype(BF16)
        both = dot(onehot[...], top) + dot(onehot[...], rest)
        put_words(1, t, words_of(both, warm_factor))
        return carry

    lax.fori_loop(0, B, pack_warm, 0)
    send_field(1)

    def pack_heat(t, carry):
        both = dot(onehot[...], heat_in[:, pl.ds(pl.multiple_of(t * PLANE, PLANE), PLANE)])
        put_words(2, t, words_of(both, heat_factor))
        return carry

    lax.fori_loop(0, B, pack_heat, 0)
    send_field(2)

    swaps, flip_rows, flip_cols, linked = [], [], [], []
    ways = []
    sources = []
    for f in range(6):
        tile = tile_ref[f : f + 1, :]
        turn = turn_ref[f : f + 1, :]
        owner = tile >> 7
        inside = tile & 127
        live = tile >= 0
        way = jnp.where(
            owner == me - minor,
            0,
            jnp.where(owner == me + minor, 1, jnp.where(owner == me - 1, 2, 3)),
        )
        way = jnp.where(owner == me, -1, way)
        way = jnp.where(live, way, -2)
        ways.append(way)
        source = jnp.where(way == -1, side_ref[f : f + 1, :] * lanes + inside, 6 * lanes + way * lanes + inside)
        sources.append(jnp.where(live, source, -1))
        swap = turn >> 2
        bit_0 = turn & 1
        bit_1 = (turn >> 1) & 1
        swaps.append(jnp.broadcast_to(swap, (B, lanes)) > 0)
        flip_rows.append(jnp.broadcast_to(jnp.where(swap > 0, bit_1, bit_0), (B, lanes)) > 0)
        flip_cols.append(jnp.broadcast_to(jnp.where(swap > 0, bit_0, bit_1), (B, lanes)) > 0)
        linked.append(jnp.broadcast_to(tile, (PLANE, lanes)) >= 0)
    square = lax.broadcasted_iota(I32, (lanes, lanes), 0)
    across = lax.broadcasted_iota(I32, (lanes, lanes), 1)
    for f in range(6):
        at = pl.ds(f * lanes, lanes)
        for n in range(10):
            gather[pl.ds(n * lanes, lanes), at] = jnp.where(
                square + n * lanes == sources[f], 1.0, 0.0
            ).astype(BF16)
        for d in range(4):
            choose[at, pl.ds(d * lanes, lanes)] = jnp.where(
                (square == across) & (ways[f] == d), 1.0, 0.0
            ).astype(BF16)
    for ref in (conduct, link_i, link_j, link_k, field_a, field_b):
        fill = jnp.full((PAD, lanes), 1.0 if ref is conduct else 0.0, F32)
        ref[pl.ds(0, PAD), :] = fill
        ref[pl.ds(PAD + CELLS, PAD), :] = fill

    neighbours = (
        (lax.rem(gx + major - 1, major), gy),
        (lax.rem(gx + 1, major), gy),
        (gx, lax.rem(gy + minor - 1, minor)),
        (gx, lax.rem(gy + 1, minor)),
    )

    def face_copies(round_):
        return [
            pltpu.make_async_remote_copy(
                leaving.at[round_, d],
                arriving.at[round_, d ^ 1],
                face_send.at[round_, d],
                face_recv.at[round_, d ^ 1],
                device_id=neighbours[d],
                device_id_type=MESH,
            )
            for d in range(4)
        ]

    def start_faces(ref, round_):
        for f in range(6):
            plain = plane_rows(ref, PAD, f)
            crossed = crossed_groups(ref, PAD, f)
            laid = [
                jnp.where(swaps[f], plain[c * B : (c + 1) * B], crossed[c]) for c in range(B)
            ]
            for c in range(B):
                turned[pl.ds(f * PLANE + c * B, B), :] = jnp.where(
                    flip_cols[f], laid[B - 1 - c], laid[c]
                )
        for f in range(6):
            back = [turned[pl.ds(f * PLANE + r, B, stride=B), :] for r in range(B)]
            plane = jnp.concatenate(
                [jnp.where(flip_rows[f], back[B - 1 - r], back[r]) for r in range(B)], axis=0
            )
            top = plane.astype(BF16)
            at = pl.ds(f * lanes, lanes)
            high[:, at] = top
            if round_ > 0:
                low[:, at] = (plane - top.astype(F32)).astype(BF16)
        for d in range(4):
            leaving[round_, d] = dot(high[...], choose[:, pl.ds(d * lanes, lanes)]).astype(BF16)
        for copy in face_copies(round_):
            copy.start()

    def finish_faces(round_, use):
        for copy in face_copies(round_):
            copy.wait()
        for pair in range(3):
            at = pl.ds(pair * 2 * lanes, 2 * lanes)
            planes = dot(high[...], gather[pl.ds(0, 6 * lanes), at])
            if round_ > 0:
                planes = planes + dot(low[...], gather[pl.ds(0, 6 * lanes), at])
            for d in range(4):
                planes = planes + dot(arriving[round_, d], gather[pl.ds((6 + d) * lanes, lanes), at])
            use(2 * pair, planes[:, :lanes])
            use(2 * pair + 1, planes[:, lanes:])

    def arrived(sems, sem, buffer):
        pltpu.make_async_copy(buffer, buffer, sems.at[sem]).wait()

    def all_but_mine(field):
        return words_got.at[field, pl.ds(0, (devices - 1) * 2 * B)]

    arrived(meta_sems, 1, meta_got.at[pl.ds(0, devices - 1)])
    meta = meta_got[...].reshape(devices, lanes)
    spread = [
        jnp.concatenate(
            [jnp.broadcast_to(meta[:, 2 * n + s : 2 * n + s + 1], (devices, lanes)) for s in range(2)],
            axis=0,
        )
        for n in range(3)
    ]
    block_id = lax.broadcasted_iota(I32, (2 * devices, lanes), 1).astype(F32)
    chosen = jnp.where(spread[0] == block_id + 1.0, 1.0, 0.0)
    warm_unit = jnp.sum(chosen * spread[1], axis=0, keepdims=True) * (1.0 / LEVELS)
    heat_unit = jnp.sum(chosen * spread[2], axis=0, keepdims=True) * (1.0 / LEVELS)
    by_block = chosen.T
    settle[:, : 2 * devices] = (by_block * 256.0).astype(BF16)
    settle[:, 2 * devices :] = by_block.astype(BF16)

    def words_at(field, t):
        words = jnp.concatenate(
            [words_got[field, pl.ds(s * B + t, devices, stride=2 * B), :] for s in range(2)], axis=0
        )
        second = (words + 32768) >> 16
        first = words - second * 65536
        return jnp.concatenate([first, second], axis=1)

    def placed_16(field, t):
        ints = words_at(field, t)
        top = ints >> 8
        rest = ints & 255
        parts = jnp.concatenate([top.astype(F32).astype(BF16), rest.astype(F32).astype(BF16)], axis=0)
        return dot(settle[...], parts).T

    depth = depth_ref[...]
    level = jnp.where(depth == 0, 1.0, jnp.where(depth == 1, 4.0, 16.0)) * (1.0 / 256.0)

    def rows_of(t):
        return pl.ds(pl.multiple_of(PAD + t * PLANE, PLANE), PLANE)

    arrived(recv_sems, 0, all_but_mine(0))

    def place_kappa(t, carry):
        ints = words_at(0, t).astype(F32).astype(BF16)
        conduct[rows_of(t), :] = dot(settle[:, 2 * devices :], ints).T * level
        return carry

    lax.fori_loop(0, B, place_kappa, 0)
    start_faces(conduct, 0)

    row_in = lax.broadcasted_iota(I32, (CHUNK, lanes), 0)
    inner_k = (row_in & (B - 1)) < B - 1
    chunks = CELLS // CHUNK

    def at_chunk(n, shift=0):
        return pl.ds(pl.multiple_of(PAD + n * CHUNK, CHUNK) + shift, CHUNK)

    def make_links(n, carry):
        here = conduct[at_chunk(n), :]
        row = row_in + n * CHUNK
        link_i[at_chunk(n), :] = jnp.where(
            row < CELLS - PLANE, harmonic(here, conduct[at_chunk(n, PLANE), :]), 0.0
        )
        link_j[at_chunk(n), :] = jnp.where(
            (row & (PLANE - 1)) < PLANE - B, harmonic(here, conduct[at_chunk(n, B), :]), 0.0
        )
        link_k[at_chunk(n), :] = jnp.where(inner_k, harmonic(here, conduct[at_chunk(n, 1), :]), 0.0)
        return carry

    lax.fori_loop(0, chunks, make_links, 0)

    def add_links(n, carry):
        inverse[at_chunk(n), :] = (
            MASS_TERM
            + link_i[at_chunk(n), :]
            + link_i[at_chunk(n, -PLANE), :]
            + link_j[at_chunk(n), :]
            + link_j[at_chunk(n, -B), :]
            + link_k[at_chunk(n), :]
            + link_k[at_chunk(n, -1), :]
        )
        return carry

    lax.fori_loop(0, chunks, add_links, 0)

    def make_face_links(f, planes):
        links = jnp.where(
            linked[f], harmonic(plane_rows(conduct, PAD, f), jnp.where(linked[f], planes, 1.0)), 0.0
        )
        face_link[f] = links
        face_update(inverse, PAD, f, links)

    finish_faces(0, make_face_links)

    def invert(n, carry):
        inverse[at_chunk(n), :] = 1.0 / inverse[at_chunk(n), :]
        return carry

    lax.fori_loop(0, chunks, invert, 0)
    for f in range(6):
        face_link[f] = face_link[f] * plane_rows(inverse, PAD, f)

    arrived(recv_sems, 1, all_but_mine(1))

    def place_warm(t, carry):
        field_a[rows_of(t), :] = placed_16(1, t) * warm_unit
        return carry

    lax.fori_loop(0, B, place_warm, 0)
    start_faces(field_a, 1)

    arrived(recv_sems, 2, all_but_mine(2))

    def place_heat(t, carry):
        right[rows_of(t), :] = MASS_TERM * (field_a[rows_of(t), :] + placed_16(2, t) * heat_unit)
        return carry

    lax.fori_loop(0, B, place_heat, 0)

    centre = 0.5 * (UPPER_BOUND + LOWER_BOUND)
    half_width = 0.5 * (UPPER_BOUND - LOWER_BOUND)
    relative = centre / half_width
    ratio = 1.0 / relative
    now, then = field_a, field_b
    for sweep in range(SWEEPS):
        if sweep == 0:
            keep, gain = 0.0, 1.0 / centre
        else:
            ratio_next = 1.0 / (2.0 * relative - ratio)
            keep, gain = ratio_next * ratio, 2.0 * ratio_next / half_width
            ratio = ratio_next
            start_faces(now, sweep + 1)

        def relax(n, carry, now=now, then=then, keep=keep, gain=gain, sweep=sweep):
            here = now[at_chunk(n), :]
            pulled = (
                right[at_chunk(n), :]
                + link_i[at_chunk(n), :] * now[at_chunk(n, PLANE), :]
                + link_i[at_chunk(n, -PLANE), :] * now[at_chunk(n, -PLANE), :]
                + link_j[at_chunk(n), :] * now[at_chunk(n, B), :]
                + link_j[at_chunk(n, -B), :] * now[at_chunk(n, -B), :]
                + link_k[at_chunk(n), :] * now[at_chunk(n, 1), :]
                + link_k[at_chunk(n, -1), :] * now[at_chunk(n, -1), :]
            )
            step = gain * (pulled * inverse[at_chunk(n), :] - here)
            if sweep > 0:
                step = step + keep * change[at_chunk(n), :]
            if sweep < SWEEPS - 1:
                change[at_chunk(n), :] = step
            then[at_chunk(n), :] = here + step
            return carry

        lax.fori_loop(0, chunks, relax, 0)

        def add_faces(f, planes, then=then, gain=gain, sweep=sweep):
            added = gain * face_link[f] * planes
            face_update(then, PAD, f, added)
            if sweep < SWEEPS - 1:
                face_update(change, PAD, f, added)

        finish_faces(sweep + 1, add_faces)
        now, then = then, now

    def write_out(t, carry):
        out_ref[:, pl.ds(pl.multiple_of(t * PLANE, PLANE), PLANE)] = now[rows_of(t), :].T
        return carry

    lax.fori_loop(0, B, write_out, 0)

    arrived(meta_sems, 0, meta_out.at[pl.ds(0, devices - 1)])
    for field in range(3):
        arrived(send_sems, field, words_out.at[field, pl.ds(0, (devices - 1) * 2 * B)])


def local(place, warmth, forcing, kappa, depth, tile, side, turn, devices, minor):
    slots = place.shape[0]
    blocks = depth.shape[0]
    lanes = 128
    tall = CELLS + 2 * PAD
    vmem = pl.BlockSpec(memory_space=pltpu.VMEM)
    hbm = pl.BlockSpec(memory_space=pl.ANY)
    tall_field = pltpu.VMEM((tall, lanes), F32)
    return pl.pallas_call(
        functools.partial(kernel, devices, minor),
        out_shape=jax.ShapeDtypeStruct((blocks, CELLS), F32),
        in_specs=[vmem] * 5 + [hbm] * 3,
        out_specs=vmem,
        scratch_shapes=[
            pltpu.VMEM((slots, CELLS), F32),
            pltpu.VMEM((slots, CELLS), BF16),
            pltpu.VMEM((slots, CELLS), BF16),
            pltpu.VMEM((devices, 1, lanes), F32),
            pltpu.VMEM((devices, 1, lanes), F32),
            pltpu.VMEM((3, devices * 2 * B, lanes), I32),
            pltpu.VMEM((3, devices * 2 * B, lanes), I32),
            pltpu.VMEM((slots, slots), BF16),
            pltpu.VMEM((blocks, 4 * devices), BF16),
            tall_field,
            tall_field,
            tall_field,
            tall_field,
            tall_field,
            tall_field,
            tall_field,
            tall_field,
            tall_field,
            pltpu.VMEM((10 * lanes, 6 * lanes), BF16),
            pltpu.VMEM((6 * lanes, 4 * lanes), BF16),
            pltpu.VMEM((6 * PLANE, lanes), F32),
            pltpu.VMEM((PLANE, 6 * lanes), BF16),
            pltpu.VMEM((PLANE, 6 * lanes), BF16),
            pltpu.VMEM((SWEEPS + 1, 4, PLANE, lanes), BF16),
            pltpu.VMEM((SWEEPS + 1, 4, PLANE, lanes), BF16),
            pltpu.VMEM((6, PLANE, lanes), F32),
            pltpu.SemaphoreType.DMA((3,)),
            pltpu.SemaphoreType.DMA((2,)),
            pltpu.SemaphoreType.DMA((3,)),
            pltpu.SemaphoreType.DMA((3,)),
            pltpu.SemaphoreType.DMA((SWEEPS + 1, 4)),
            pltpu.SemaphoreType.DMA((SWEEPS + 1, 4)),
        ],
        compiler_params=pltpu.CompilerParams(
            collective_id=0, has_side_effects=True, vmem_limit_bytes=60 * 2**20
        ),
    )(
        place.reshape(1, slots),
        depth.reshape(1, blocks),
        tile,
        side,
        turn,
        warmth,
        forcing,
        kappa,
    )


def solution(mesh):
    both = ("gx", "gy")
    devices = mesh.shape["gx"] * mesh.shape["gy"]
    return jax.shard_map(
        functools.partial(local, devices=devices, minor=mesh.shape["gy"]),
        mesh=mesh,
        in_specs=(
            P(both),
            P(both, None),
            P(both, None),
            P(both, None),
            P(both),
            P(None, both),
            P(None, both),
            P(None, both),
        ),
        out_specs=P(both, None),
        check_vma=False,
    )
```

profile of v0, /device:TPU:1, one launch (start us, length us, event | category | flops | bytes accessed | tf_op | source)
XLA Modules:
  0.0 130.7 jit_solution(6226631174330804888)
XLA Ops:
  0.0 127.6 %shard_map.82 = f32[128,4096]{1,0:T(8,128)} custom-call(s32[1,256]{1,0:T(1,128)} %bitcast.2, s32[1,128]{1,0:T(1,128)} %bitcast.3, s32[6,128]{1,0:T(8,128)} %tile_ref.1, s32[6,128]{1,0:T(8,128)} %side_ref.1, s32[6,128]{1,0:T(8,128)} %turn_ref.1, f32[256,4096]{1,0:T(8,128)} %warm_hbm.1, bf16[256,4096]{1,0:T(8,128)(2,1)} %heat_hbm.1, bf16[256,4096]{1,0:T(8,128)(2,1)} %kappa_hbm.1), custom_call_target="tpu_custom_call" | custom-call | tf_op jit(solution)/shard_map/pallas_call | solution.py:542
  127.6 3.1 %copy.10 = f32[128,4096]{1,0:T(8,128)} copy(f32[128,4096]{1,0:T(8,128)} %shard_map.82) | data formatting | bytes 4194304
where the time goes:
time: 133 us; the launch traced here: 131 us
  Pallas kernels  128 us (96%)
  local copies, waits for them, and re-layouts  3.11 us (2%)
    pallas_call x1, Pallas kernels, local(): pl.pallas_call(functools.partial(kernel, devices, minor), out_shape=jax.S...  128 us
    unnamed x1, local copies, waits for them, and re-layouts  3.11 us

commit v1 on v0

--- a/solution.py
+++ b/solution.py
@@ -14,7 +14,10 @@
 MASS_TERM = 4.0
 LOWER_BOUND = 0.25
 UPPER_BOUND = 2.0
-CHUNK = 128
+CHUNK = 64
+PARTS = 4
+PLANES = B // PARTS
+EARLY = 2
 PAD = PLANE
 LEVELS = 32767.0
 F32 = jnp.float32
@@ -85,6 +88,8 @@
     meta_got,
     words_out,
     words_got,
+    heat_out,
+    heat_got,
     onehot,
     settle,
     conduct,
@@ -104,10 +109,13 @@
     leaving,
     arriving,
     face_link,
+    near,
     load_sem,
     meta_sems,
     send_sems,
     recv_sems,
+    part_send,
+    part_recv,
     face_send,
     face_recv,
 ):
@@ -120,8 +128,8 @@
     barrier = pltpu.get_barrier_semaphore()
 
     def peer(t):
-        p = lax.rem(me + t, devices)
-        return p, (p // minor, lax.rem(p, minor))
+        p = lax.rem(me + t * 37, devices)
+        return p, (lax.div(p, minor), lax.rem(p, minor))
 
     def greet(t, carry):
         pl.semaphore_signal(barrier, inc=1, device_id=peer(t)[1], device_id_type=MESH)
@@ -151,38 +159,46 @@
     tag_col = jnp.where(place_col >= 0.0, place_col - owner_col * lanes + 1.0, 0.0)
     tags = dot(onehot[...], jnp.broadcast_to(tag_col, (slots, lanes)).astype(BF16))
 
-    def put_words(field, t, words):
+    def put_words(ref, field, t, planes, words):
         for s in range(2):
-            words_out[field, pl.ds(s * B + t, devices, stride=2 * B), :] = words[
+            ref[field, pl.ds(s * planes + t, devices, stride=2 * planes), :] = words[
                 s * devices : (s + 1) * devices
             ]
 
-    def send_field(field):
+    def send_words(out, got, field, rows, sem_out, sem_got):
+        def block(p):
+            return pl.ds(pl.multiple_of(p * rows, rows), rows)
+
         def one(t, carry):
             p, where = peer(t)
             pltpu.make_async_remote_copy(
-                words_out.at[field, pl.ds(pl.multiple_of(p * 2 * B, 2 * B), 2 * B)],
-                words_got.at[field, pl.ds(pl.multiple_of(me * 2 * B, 2 * B), 2 * B)],
-                send_sems.at[field],
-                recv_sems.at[field],
+                out.at[field, block(p)],
+                got.at[field, block(me)],
+                sem_out.at[field],
+                sem_got.at[field],
                 device_id=where,
                 device_id_type=MESH,
             ).start()
             return carry
 
         lax.fori_loop(1, devices, one, 0)
-        mine = pl.ds(pl.multiple_of(me * 2 * B, 2 * B), 2 * B)
-        words_got[field, mine, :] = words_out[field, mine, :]
+        got[field, block(me), :] = out[field, block(me), :]
+
+    def send_field(field):
+        send_words(words_out, words_got, field, 2 * B, send_sems, recv_sems)
+
+    def send_part(part):
+        send_words(heat_out, heat_got, part, 2 * PLANES, part_send, part_recv)
 
     loads[0].wait()
 
     def pack_kappa(t, carry):
         both = dot(onehot[...], kappa_in[:, pl.ds(pl.multiple_of(t * PLANE, PLANE), PLANE)])
         ints = (both * 256.0).astype(I32)
-        put_words(0, t, ints[:, :lanes] + ints[:, lanes:] * 65536)
-        return carry
-
-    lax.fori_loop(0, B, pack_kappa, 0)
+        put_words(words_out, 0, t, B, ints[:, :lanes] + ints[:, lanes:] * 65536)
+        return carry
+
+    lax.fori_loop(0, B, pack_kappa, 0, unroll=2)
     pl.semaphore_wait(barrier, devices - 1)
     send_field(0)
 
@@ -237,19 +253,20 @@
         top = value.astype(BF16)
         rest = (value - top.astype(F32)).astype(BF16)
         both = dot(onehot[...], top) + dot(onehot[...], rest)
-        put_words(1, t, words_of(both, warm_factor))
-        return carry
-
-    lax.fori_loop(0, B, pack_warm, 0)
+        put_words(words_out, 1, t, B, words_of(both, warm_factor))
+        return carry
+
+    lax.fori_loop(0, B, pack_warm, 0, unroll=2)
     send_field(1)
 
     def pack_heat(t, carry):
         both = dot(onehot[...], heat_in[:, pl.ds(pl.multiple_of(t * PLANE, PLANE), PLANE)])
-        put_words(2, t, words_of(both, heat_factor))
-        return carry
-
-    lax.fori_loop(0, B, pack_heat, 0)
-    send_field(2)
+        put_words(heat_out, t // PLANES, t % PLANES, PLANES, words_of(both, heat_factor))
+        return carry
+
+    lax.fori_loop(0, B, pack_heat, 0, unroll=2)
+    for part in range(EARLY):
+        send_part(part)
 
     swaps, flip_rows, flip_cols, linked = [], [], [], []
     ways = []
@@ -332,24 +349,27 @@
             )
             top = plane.astype(BF16)
             at = pl.ds(f * lanes, lanes)
-            high[:, at] = top
+            high[min(round_, 1), :, at] = top
             if round_ > 0:
                 low[:, at] = (plane - top.astype(F32)).astype(BF16)
         for d in range(4):
-            leaving[round_, d] = dot(high[...], choose[:, pl.ds(d * lanes, lanes)]).astype(BF16)
+            leaving[round_, d] = dot(high[min(round_, 1)], choose[:, pl.ds(d * lanes, lanes)]).astype(BF16)
         for copy in face_copies(round_):
             copy.start()
 
     def finish_faces(round_, use):
-        for copy in face_copies(round_):
-            copy.wait()
         for pair in range(3):
             at = pl.ds(pair * 2 * lanes, 2 * lanes)
-            planes = dot(high[...], gather[pl.ds(0, 6 * lanes), at])
+            planes = dot(high[min(round_, 1)], gather[pl.ds(0, 6 * lanes), at])
             if round_ > 0:
                 planes = planes + dot(low[...], gather[pl.ds(0, 6 * lanes), at])
-            for d in range(4):
-                planes = planes + dot(arriving[round_, d], gather[pl.ds((6 + d) * lanes, lanes), at])
+            near[:, at] = planes
+        for copy in face_copies(round_):
+            copy.wait_recv()
+        far = jnp.concatenate([arriving[round_, d] for d in range(4)], axis=1)
+        for pair in range(3):
+            at = pl.ds(pair * 2 * lanes, 2 * lanes)
+            planes = near[:, at] + dot(far, gather[pl.ds(6 * lanes, 4 * lanes), at])
             use(2 * pair, planes[:, :lanes])
             use(2 * pair + 1, planes[:, lanes:])
 
@@ -371,21 +391,21 @@
     block_id = lax.broadcasted_iota(I32, (2 * devices, lanes), 1).astype(F32)
     chosen = jnp.where(spread[0] == block_id + 1.0, 1.0, 0.0)
     warm_unit = jnp.sum(chosen * spread[1], axis=0, keepdims=True) * (1.0 / LEVELS)
-    heat_unit = jnp.sum(chosen * spread[2], axis=0, keepdims=True) * (1.0 / LEVELS)
+    heat_scale_row = jnp.sum(chosen * spread[2], axis=0, keepdims=True) * (MASS_TERM / LEVELS)
     by_block = chosen.T
     settle[:, : 2 * devices] = (by_block * 256.0).astype(BF16)
     settle[:, 2 * devices :] = by_block.astype(BF16)
 
-    def words_at(field, t):
+    def words_at(ref, field, t, planes):
         words = jnp.concatenate(
-            [words_got[field, pl.ds(s * B + t, devices, stride=2 * B), :] for s in range(2)], axis=0
+            [ref[field, pl.ds(s * planes + t, devices, stride=2 * planes), :] for s in range(2)], axis=0
         )
         second = (words + 32768) >> 16
         first = words - second * 65536
         return jnp.concatenate([first, second], axis=1)
 
-    def placed_16(field, t):
-        ints = words_at(field, t)
+    def placed_16(ref, field, t, planes):
+        ints = words_at(ref, field, t, planes)
         top = ints >> 8
         rest = ints & 255
         parts = jnp.concatenate([top.astype(F32).astype(BF16), rest.astype(F32).astype(BF16)], axis=0)
@@ -400,12 +420,14 @@
     arrived(recv_sems, 0, all_but_mine(0))
 
     def place_kappa(t, carry):
-        ints = words_at(0, t).astype(F32).astype(BF16)
+        ints = words_at(words_got, 0, t, B).astype(F32).astype(BF16)
         conduct[rows_of(t), :] = dot(settle[:, 2 * devices :], ints).T * level
         return carry
 
-    lax.fori_loop(0, B, place_kappa, 0)
+    lax.fori_loop(0, B, place_kappa, 0, unroll=2)
     start_faces(conduct, 0)
+    for part in range(EARLY, PARTS):
+        send_part(part)
 
     row_in = lax.broadcasted_iota(I32, (CHUNK, lanes), 0)
     inner_k = (row_in & (B - 1)) < B - 1
@@ -426,7 +448,7 @@
         link_k[at_chunk(n), :] = jnp.where(inner_k, harmonic(here, conduct[at_chunk(n, 1), :]), 0.0)
         return carry
 
-    lax.fori_loop(0, chunks, make_links, 0)
+    lax.fori_loop(0, chunks, make_links, 0, unroll=2)
 
     def add_links(n, carry):
         inverse[at_chunk(n), :] = (
@@ -440,7 +462,32 @@
         )
         return carry
 
-    lax.fori_loop(0, chunks, add_links, 0)
+    lax.fori_loop(0, chunks, add_links, 0, unroll=2)
+
+    arrived(recv_sems, 1, all_but_mine(1))
+
+    def place_warm(t, carry):
+        field_a[rows_of(t), :] = placed_16(words_got, 1, t, B) * warm_unit
+        return carry
+
+    lax.fori_loop(0, B, place_warm, 0, unroll=2)
+    start_faces(field_a, 1)
+
+    def inner_sum(now, n):
+        return (
+            link_i[at_chunk(n), :] * now[at_chunk(n, PLANE), :]
+            + link_i[at_chunk(n, -PLANE), :] * now[at_chunk(n, -PLANE), :]
+            + link_j[at_chunk(n), :] * now[at_chunk(n, B), :]
+            + link_j[at_chunk(n, -B), :] * now[at_chunk(n, -B), :]
+            + link_k[at_chunk(n), :] * now[at_chunk(n, 1), :]
+            + link_k[at_chunk(n, -1), :] * now[at_chunk(n, -1), :]
+        )
+
+    def first_sum(n, carry):
+        change[at_chunk(n), :] = MASS_TERM * field_a[at_chunk(n), :] + inner_sum(field_a, n)
+        return carry
+
+    lax.fori_loop(0, chunks, first_sum, 0, unroll=2)
 
     def make_face_links(f, planes):
         links = jnp.where(
@@ -455,61 +502,51 @@
         inverse[at_chunk(n), :] = 1.0 / inverse[at_chunk(n), :]
         return carry
 
-    lax.fori_loop(0, chunks, invert, 0)
-    for f in range(6):
+    lax.fori_loop(0, chunks, invert, 0, unroll=2)
+
+    def first_faces(f, planes):
+        face_update(change, PAD, f, face_link[f] * planes)
         face_link[f] = face_link[f] * plane_rows(inverse, PAD, f)
 
-    arrived(recv_sems, 1, all_but_mine(1))
-
-    def place_warm(t, carry):
-        field_a[rows_of(t), :] = placed_16(1, t) * warm_unit
-        return carry
-
-    lax.fori_loop(0, B, place_warm, 0)
-    start_faces(field_a, 1)
-
-    arrived(recv_sems, 2, all_but_mine(2))
-
-    def place_heat(t, carry):
-        right[rows_of(t), :] = MASS_TERM * (field_a[rows_of(t), :] + placed_16(2, t) * heat_unit)
-        return carry
-
-    lax.fori_loop(0, B, place_heat, 0)
+    finish_faces(1, first_faces)
 
     centre = 0.5 * (UPPER_BOUND + LOWER_BOUND)
     half_width = 0.5 * (UPPER_BOUND - LOWER_BOUND)
     relative = centre / half_width
     ratio = 1.0 / relative
-    now, then = field_a, field_b
-    for sweep in range(SWEEPS):
-        if sweep == 0:
-            keep, gain = 0.0, 1.0 / centre
-        else:
-            ratio_next = 1.0 / (2.0 * relative - ratio)
-            keep, gain = ratio_next * ratio, 2.0 * ratio_next / half_width
-            ratio = ratio_next
-            start_faces(now, sweep + 1)
+
+    for part in range(PARTS):
+        arrived(part_recv, part, heat_got.at[part, pl.ds(0, (devices - 1) * 2 * PLANES)])
+
+        def place_heat(t, carry, part=part):
+            at = rows_of(t + part * PLANES)
+            here = field_a[at, :]
+            added = placed_16(heat_got, part, t, PLANES) * heat_scale_row
+            right[at, :] = MASS_TERM * here + added
+            step = (1.0 / centre) * ((change[at, :] + added) * inverse[at, :] - here)
+            change[at, :] = step
+            field_b[at, :] = here + step
+            return carry
+
+        lax.fori_loop(0, PLANES, place_heat, 0, unroll=2)
+
+    now, then = field_b, field_a
+    for sweep in range(1, SWEEPS):
+        ratio_next = 1.0 / (2.0 * relative - ratio)
+        keep, gain = ratio_next * ratio, 2.0 * ratio_next / half_width
+        ratio = ratio_next
+        start_faces(now, sweep + 1)
 
         def relax(n, carry, now=now, then=then, keep=keep, gain=gain, sweep=sweep):
             here = now[at_chunk(n), :]
-            pulled = (
-                right[at_chunk(n), :]
-                + link_i[at_chunk(n), :] * now[at_chunk(n, PLANE), :]
-                + link_i[at_chunk(n, -PLANE), :] * now[at_chunk(n, -PLANE), :]
-                + link_j[at_chunk(n), :] * now[at_chunk(n, B), :]
-                + link_j[at_chunk(n, -B), :] * now[at_chunk(n, -B), :]
-                + link_k[at_chunk(n), :] * now[at_chunk(n, 1), :]
-                + link_k[at_chunk(n, -1), :] * now[at_chunk(n, -1), :]
-            )
-            step = gain * (pulled * inverse[at_chunk(n), :] - here)
-            if sweep > 0:
-                step = step + keep * change[at_chunk(n), :]
+            pulled = right[at_chunk(n), :] + inner_sum(now, n)
+            step = gain * (pulled * inverse[at_chunk(n), :] - here) + keep * change[at_chunk(n), :]
             if sweep < SWEEPS - 1:
                 change[at_chunk(n), :] = step
             then[at_chunk(n), :] = here + step
             return carry
 
-        lax.fori_loop(0, chunks, relax, 0)
+        lax.fori_loop(0, chunks, relax, 0, unroll=2)
 
         def add_faces(f, planes, then=then, gain=gain, sweep=sweep):
             added = gain * face_link[f] * planes
@@ -524,11 +561,16 @@
         out_ref[:, pl.ds(pl.multiple_of(t * PLANE, PLANE), PLANE)] = now[rows_of(t), :].T
         return carry
 
-    lax.fori_loop(0, B, write_out, 0)
-
+    lax.fori_loop(0, B, write_out, 0, unroll=2)
+
+    for round_ in range(SWEEPS + 1):
+        for copy in face_copies(round_):
+            copy.wait_send()
     arrived(meta_sems, 0, meta_out.at[pl.ds(0, devices - 1)])
-    for field in range(3):
+    for field in range(2):
         arrived(send_sems, field, words_out.at[field, pl.ds(0, (devices - 1) * 2 * B)])
+    for part in range(PARTS):
+        arrived(part_send, part, heat_out.at[part, pl.ds(0, (devices - 1) * 2 * PLANES)])
 
 
 def local(place, warmth, forcing, kappa, depth, tile, side, turn, devices, minor):
@@ -541,7 +583,7 @@
     tall_field = pltpu.VMEM((tall, lanes), F32)
     return pl.pallas_call(
         functools.partial(kernel, devices, minor),
-        out_shape=jax.ShapeDtypeStruct((blocks, CELLS), F32),
+        out_shape=pltpu.VMEM((blocks, CELLS), F32),
         in_specs=[vmem] * 5 + [hbm] * 3,
         out_specs=vmem,
         scratch_shapes=[
@@ -550,8 +592,10 @@
             pltpu.VMEM((slots, CELLS), BF16),
             pltpu.VMEM((devices, 1, lanes), F32),
             pltpu.VMEM((devices, 1, lanes), F32),
-            pltpu.VMEM((3, devices * 2 * B, lanes), I32),
-            pltpu.VMEM((3, devices * 2 * B, lanes), I32),
+            pltpu.VMEM((2, devices * 2 * B, lanes), I32),
+            pltpu.VMEM((2, devices * 2 * B, lanes), I32),
+            pltpu.VMEM((PARTS, devices * 2 * PLANES, lanes), I32),
+            pltpu.VMEM((PARTS, devices * 2 * PLANES, lanes), I32),
             pltpu.VMEM((slots, slots), BF16),
             pltpu.VMEM((blocks, 4 * devices), BF16),
             tall_field,
@@ -566,20 +610,23 @@
             pltpu.VMEM((10 * lanes, 6 * lanes), BF16),
             pltpu.VMEM((6 * lanes, 4 * lanes), BF16),
             pltpu.VMEM((6 * PLANE, lanes), F32),
-            pltpu.VMEM((PLANE, 6 * lanes), BF16),
+            pltpu.VMEM((2, PLANE, 6 * lanes), BF16),
             pltpu.VMEM((PLANE, 6 * lanes), BF16),
             pltpu.VMEM((SWEEPS + 1, 4, PLANE, lanes), BF16),
             pltpu.VMEM((SWEEPS + 1, 4, PLANE, lanes), BF16),
             pltpu.VMEM((6, PLANE, lanes), F32),
+            pltpu.VMEM((PLANE, 6 * lanes), F32),
             pltpu.SemaphoreType.DMA((3,)),
             pltpu.SemaphoreType.DMA((2,)),
-            pltpu.SemaphoreType.DMA((3,)),
-            pltpu.SemaphoreType.DMA((3,)),
+            pltpu.SemaphoreType.DMA((2,)),
+            pltpu.SemaphoreType.DMA((2,)),
+            pltpu.SemaphoreType.DMA((PARTS,)),
+            pltpu.SemaphoreType.DMA((PARTS,)),
             pltpu.SemaphoreType.DMA((SWEEPS + 1, 4)),
             pltpu.SemaphoreType.DMA((SWEEPS + 1, 4)),
         ],
         compiler_params=pltpu.CompilerParams(
-            collective_id=0, has_side_effects=True, vmem_limit_bytes=60 * 2**20
+            collective_id=0, has_side_effects=True, vmem_limit_bytes=54 * 2**20
         ),
     )(
         place.reshape(1, slots),

time: 133 us -> 106 us (0.80); the launches traced: 131 us -> 106 us
  Pallas kernels: 128 us -> 104 us
  local copies, waits for them, and re-layouts: 3.11 us -> 1.32 us
    pallas_call x1, Pallas kernels: 128 us -> 104 us  [local(): pl.pallas_call(functools.partial(kernel, devices, minor), out_shape=pltpu...]
    unnamed x1, local copies, waits for them, and re-layouts: 3.11 us -> 1.32 us
where the time goes in v1:
time: 106 us
  Pallas kernels  104 us (98%)
  local copies, waits for them, and re-layouts  1.32 us (1%)
    pallas_call x1, Pallas kernels, local(): pl.pallas_call(functools.partial(kernel, devices, minor), out_shape=pltpu...  104 us

profile of v1, /device:TPU:1, one launch (start us, length us, event | category | flops | bytes accessed | tf_op | source)
XLA Modules:
  0.0 105.6 jit_solution(10778152545118538209)
XLA Ops:
  0.0 104.3 %shard_map.82 = f32[128,4096]{1,0:T(8,128)S(1)} custom-call(s32[1,256]{1,0:T(1,128)} %bitcast.2, s32[1,128]{1,0:T(1,128)} %bitcast.3, s32[6,128]{1,0:T(8,128)} %tile_ref.1, s32[6,128]{1,0:T(8,128)} %side_ref.1, s32[6,128]{1,0:T(8,128)} %turn_ref.1, f32[256,4096]{1,0:T(8,128)} %warm_hbm.1, bf16[256,4096]{1,0:T(8,128)(2,1)} %heat_hbm.1, ...), custom_call_target="tpu_custom_call" | custom-call | tf_op jit(solution)/shard_map/pallas_call | solution.py:584
  104.3 1.3 %copy.10 = f32[128,4096]{1,0:T(8,128)} copy(f32[128,4096]{1,0:T(8,128)S(1)} %shard_map.82) | data formatting | bytes 4194304

commit v2 on v1

--- a/solution.py
+++ b/solution.py
@@ -16,8 +16,10 @@
 UPPER_BOUND = 2.0
 CHUNK = 64
 PARTS = 4
+FACE_CAP = 32
 PLANES = B // PARTS
 EARLY = 2
+LATE = 3
 PAD = PLANE
 LEVELS = 32767.0
 F32 = jnp.float32
@@ -104,6 +106,7 @@
     gather,
     choose,
     turned,
+    picked,
     high,
     low,
     leaving,
@@ -270,7 +273,8 @@
 
     swaps, flip_rows, flip_cols, linked = [], [], [], []
     ways = []
-    sources = []
+    insides = []
+    turn_bits = []
     for f in range(6):
         tile = tile_ref[f : f + 1, :]
         turn = turn_ref[f : f + 1, :]
@@ -285,27 +289,62 @@
         way = jnp.where(owner == me, -1, way)
         way = jnp.where(live, way, -2)
         ways.append(way)
-        source = jnp.where(way == -1, side_ref[f : f + 1, :] * lanes + inside, 6 * lanes + way * lanes + inside)
-        sources.append(jnp.where(live, source, -1))
+        insides.append(inside)
         swap = turn >> 2
         bit_0 = turn & 1
         bit_1 = (turn >> 1) & 1
+        turn_bits.append(
+            [swap, jnp.where(swap > 0, bit_1, bit_0), jnp.where(swap > 0, bit_0, bit_1)]
+        )
         swaps.append(jnp.broadcast_to(swap, (B, lanes)) > 0)
         flip_rows.append(jnp.broadcast_to(jnp.where(swap > 0, bit_1, bit_0), (B, lanes)) > 0)
         flip_cols.append(jnp.broadcast_to(jnp.where(swap > 0, bit_0, bit_1), (B, lanes)) > 0)
         linked.append(jnp.broadcast_to(tile, (PLANE, lanes)) >= 0)
     square = lax.broadcasted_iota(I32, (lanes, lanes), 0)
     across = lax.broadcasted_iota(I32, (lanes, lanes), 1)
+    def column(row):
+        return jnp.sum(jnp.where(square == across, row, 0.0), axis=1, keepdims=True)
+
+    def below(counts, limit):
+        return jnp.sum(jnp.where(square < limit, counts, 0.0), axis=0, keepdims=True)
+
+    ranks, theirs = [], []
+    for d in range(4):
+        sends = sum(jnp.where(ways[f] == d, 1.0, 0.0) for f in range(6))
+        ranks.append(below(column(sends), across))
+        marks = sum(
+            jnp.where((square == insides[f]) & (ways[f] == d), 1.0, 0.0) for f in range(6)
+        )
+        theirs.append(jnp.sum(marks, axis=1, keepdims=True))
     for f in range(6):
         at = pl.ds(f * lanes, lanes)
+        source = jnp.where(
+            ways[f] == -1, (side_ref[f : f + 1, :] * lanes + insides[f]).astype(F32), -1.0
+        )
+        lane = jnp.full((1, lanes), -1.0, F32)
+        for d in range(4):
+            slot = below(theirs[d], insides[f])
+            source = jnp.where(ways[f] == d, (6 + d) * lanes + (d ^ 1) * FACE_CAP + slot, source)
+            lane = jnp.where(ways[f] == d, d * FACE_CAP + ranks[d], lane)
+        source = source.astype(I32)
         for n in range(10):
             gather[pl.ds(n * lanes, lanes), at] = jnp.where(
-                square + n * lanes == sources[f], 1.0, 0.0
+                square + n * lanes == source, 1.0, 0.0
             ).astype(BF16)
-        for d in range(4):
-            choose[at, pl.ds(d * lanes, lanes)] = jnp.where(
-                (square == across) & (ways[f] == d), 1.0, 0.0
-            ).astype(BF16)
+        choose[at, :] = jnp.where(column(lane) == across.astype(F32), 1.0, 0.0).astype(BF16)
+    sent_bits = [
+        jnp.broadcast_to(
+            dot(
+                jnp.concatenate(
+                    [jnp.broadcast_to(turn_bits[f][n], (B, lanes)) for f in range(6)], axis=1
+                ).astype(F32).astype(BF16),
+                choose[...],
+            ),
+            (B, lanes),
+        )
+        > 0.5
+        for n in range(3)
+    ]
     for ref in (conduct, link_i, link_j, link_k, field_a, field_b):
         fill = jnp.full((PAD, lanes), 1.0 if ref is conduct else 0.0, F32)
         ref[pl.ds(0, PAD), :] = fill
@@ -321,7 +360,7 @@
     def face_copies(round_):
         return [
             pltpu.make_async_remote_copy(
-                leaving.at[round_, d],
+                leaving.at[round_],
                 arriving.at[round_, d ^ 1],
                 face_send.at[round_, d],
                 face_recv.at[round_, d ^ 1],
@@ -331,31 +370,43 @@
             for d in range(4)
         ]
 
+    def turn_planes(plain, crossed, scratch, swap, flip_col):
+        laid = [jnp.where(swap, plain[c * B : (c + 1) * B], crossed[c]) for c in range(B)]
+        for c in range(B):
+            scratch[pl.ds(c * B, B), :] = jnp.where(flip_col, laid[B - 1 - c], laid[c])
+
+    def turned_back(scratch, flip_row):
+        back = [scratch[pl.ds(r, B, stride=B), :] for r in range(B)]
+        return jnp.concatenate(
+            [jnp.where(flip_row, back[B - 1 - r], back[r]) for r in range(B)], axis=0
+        )
+
     def start_faces(ref, round_):
+        which = min(round_, 1)
         for f in range(6):
-            plain = plane_rows(ref, PAD, f)
-            crossed = crossed_groups(ref, PAD, f)
-            laid = [
-                jnp.where(swaps[f], plain[c * B : (c + 1) * B], crossed[c]) for c in range(B)
-            ]
-            for c in range(B):
-                turned[pl.ds(f * PLANE + c * B, B), :] = jnp.where(
-                    flip_cols[f], laid[B - 1 - c], laid[c]
-                )
+            low[:, pl.ds(f * lanes, lanes)] = plane_rows(ref, PAD, f).astype(BF16)
+        sent = dot(low[...], choose[...])
+        picked[...] = sent
+        crossed = [picked[pl.ds(v, B, stride=B), :] for v in range(B)]
+        turn_planes(sent, crossed, turned.at[0], sent_bits[0], sent_bits[2])
+        leaving[round_] = turned_back(turned.at[0], sent_bits[1]).astype(BF16)
+        for copy in face_copies(round_):
+            copy.start()
         for f in range(6):
-            back = [turned[pl.ds(f * PLANE + r, B, stride=B), :] for r in range(B)]
-            plane = jnp.concatenate(
-                [jnp.where(flip_rows[f], back[B - 1 - r], back[r]) for r in range(B)], axis=0
+            turn_planes(
+                plane_rows(ref, PAD, f),
+                crossed_groups(ref, PAD, f),
+                turned.at[f],
+                swaps[f],
+                flip_cols[f],
             )
+        for f in range(6):
+            plane = turned_back(turned.at[f], flip_rows[f])
             top = plane.astype(BF16)
             at = pl.ds(f * lanes, lanes)
-            high[min(round_, 1), :, at] = top
+            high[which, :, at] = top
             if round_ > 0:
                 low[:, at] = (plane - top.astype(F32)).astype(BF16)
-        for d in range(4):
-            leaving[round_, d] = dot(high[min(round_, 1)], choose[:, pl.ds(d * lanes, lanes)]).astype(BF16)
-        for copy in face_copies(round_):
-            copy.start()
 
     def finish_faces(round_, use):
         for pair in range(3):
@@ -426,7 +477,7 @@
 
     lax.fori_loop(0, B, place_kappa, 0, unroll=2)
     start_faces(conduct, 0)
-    for part in range(EARLY, PARTS):
+    for part in range(EARLY, LATE):
         send_part(part)
 
     row_in = lax.broadcasted_iota(I32, (CHUNK, lanes), 0)
@@ -472,6 +523,8 @@
 
     lax.fori_loop(0, B, place_warm, 0, unroll=2)
     start_faces(field_a, 1)
+    for part in range(LATE, PARTS):
+        send_part(part)
 
     def inner_sum(now, n):
         return (
@@ -608,11 +661,12 @@
             tall_field,
             tall_field,
             pltpu.VMEM((10 * lanes, 6 * lanes), BF16),
-            pltpu.VMEM((6 * lanes, 4 * lanes), BF16),
-            pltpu.VMEM((6 * PLANE, lanes), F32),
+            pltpu.VMEM((6 * lanes, lanes), BF16),
+            pltpu.VMEM((6, PLANE, lanes), F32),
+            pltpu.VMEM((PLANE, lanes), F32),
             pltpu.VMEM((2, PLANE, 6 * lanes), BF16),
             pltpu.VMEM((PLANE, 6 * lanes), BF16),
-            pltpu.VMEM((SWEEPS + 1, 4, PLANE, lanes), BF16),
+            pltpu.VMEM((SWEEPS + 1, PLANE, lanes), BF16),
             pltpu.VMEM((SWEEPS + 1, 4, PLANE, lanes), BF16),
             pltpu.VMEM((6, PLANE, lanes), F32),
             pltpu.VMEM((PLANE, 6 * lanes), F32),

time: 106 us -> 102 us (0.962)
  Pallas kernels: 104 us -> 100 us
    pallas_call x1, Pallas kernels: 104 us -> 100 us  [local(): pl.pallas_call(functools.partial(kernel, devices, minor), out_shape=pltpu...]
where the time goes in v2:
time: 102 us
  Pallas kernels  100 us (98%)
  local copies, waits for them, and re-layouts  1.32 us (1%)
    pallas_call x1, Pallas kernels, local(): pl.pallas_call(functools.partial(kernel, devices, minor), out_shape=pltpu...  100 us

profile of v2, /device:TPU:1, one launch (start us, length us, event | category | flops | bytes accessed | tf_op | source)
XLA Modules:
  0.0 101.8 jit_solution(1329376534161368899)
XLA Ops:
  0.0 100.4 %shard_map.82 = f32[128,4096]{1,0:T(8,128)S(1)} custom-call(s32[1,256]{1,0:T(1,128)} %bitcast.2, s32[1,128]{1,0:T(1,128)} %bitcast.3, s32[6,128]{1,0:T(8,128)} %tile_ref.1, s32[6,128]{1,0:T(8,128)} %side_ref.1, s32[6,128]{1,0:T(8,128)} %turn_ref.1, f32[256,4096]{1,0:T(8,128)} %warm_hbm.1, bf16[256,4096]{1,0:T(8,128)(2,1)} %heat_hbm.1, ...), custom_call_target="tpu_custom_call" | custom-call | tf_op jit(solution)/shard_map/pallas_call | solution.py:637
  100.5 1.3 %copy.10 = f32[128,4096]{1,0:T(8,128)} copy(f32[128,4096]{1,0:T(8,128)S(1)} %shard_map.82) | data formatting | bytes 4194304

commit v3 on v2

--- a/solution.py
+++ b/solution.py
@@ -15,11 +15,12 @@
 LOWER_BOUND = 0.25
 UPPER_BOUND = 2.0
 CHUNK = 64
-PARTS = 4
+PARTS = 8
 FACE_CAP = 32
+FOLD = PLANE // 4
 PLANES = B // PARTS
-EARLY = 2
-LATE = 3
+EARLY = 4
+LATE = 6
 PAD = PLANE
 LEVELS = 32767.0
 F32 = jnp.float32
@@ -324,10 +325,10 @@
         lane = jnp.full((1, lanes), -1.0, F32)
         for d in range(4):
             slot = below(theirs[d], insides[f])
-            source = jnp.where(ways[f] == d, (6 + d) * lanes + (d ^ 1) * FACE_CAP + slot, source)
+            source = jnp.where(ways[f] == d, 6 * lanes + d * FACE_CAP + slot, source)
             lane = jnp.where(ways[f] == d, d * FACE_CAP + ranks[d], lane)
         source = source.astype(I32)
-        for n in range(10):
+        for n in range(7):
             gather[pl.ds(n * lanes, lanes), at] = jnp.where(
                 square + n * lanes == source, 1.0, 0.0
             ).astype(BF16)
@@ -360,7 +361,7 @@
     def face_copies(round_):
         return [
             pltpu.make_async_remote_copy(
-                leaving.at[round_],
+                leaving.at[round_, d],
                 arriving.at[round_, d ^ 1],
                 face_send.at[round_, d],
                 face_recv.at[round_, d ^ 1],
@@ -381,6 +382,12 @@
             [jnp.where(flip_row, back[B - 1 - r], back[r]) for r in range(B)], axis=0
         )
 
+    quarter = lax.broadcasted_iota(I32, (FOLD, lanes), 1) >> 5
+
+    def rolled(value, quarters):
+        shift = FACE_CAP * quarters % lanes
+        return pltpu.roll(value, shift, axis=1) if shift else value
+
     def start_faces(ref, round_):
         which = min(round_, 1)
         for f in range(6):
@@ -389,7 +396,13 @@
         picked[...] = sent
         crossed = [picked[pl.ds(v, B, stride=B), :] for v in range(B)]
         turn_planes(sent, crossed, turned.at[0], sent_bits[0], sent_bits[2])
-        leaving[round_] = turned_back(turned.at[0], sent_bits[1]).astype(BF16)
+        plane = turned_back(turned.at[0], sent_bits[1])
+        for d in range(4):
+            folded = jnp.zeros((FOLD, lanes), F32)
+            for q in range(4):
+                moved = rolled(plane[q * FOLD : (q + 1) * FOLD], q - d)
+                folded = jnp.where(quarter == q, moved, folded)
+            leaving[round_, d] = folded.astype(BF16)
         for copy in face_copies(round_):
             copy.start()
         for f in range(6):
@@ -417,10 +430,17 @@
             near[:, at] = planes
         for copy in face_copies(round_):
             copy.wait_recv()
-        far = jnp.concatenate([arriving[round_, d] for d in range(4)], axis=1)
+        came = [arriving[round_, d].astype(F32) for d in range(4)]
+        unfolded = []
+        for q in range(4):
+            rows = jnp.zeros((FOLD, lanes), F32)
+            for d in range(4):
+                rows = jnp.where(quarter == d, rolled(came[d], d - q), rows)
+            unfolded.append(rows)
+        far = jnp.concatenate(unfolded, axis=0).astype(BF16)
         for pair in range(3):
             at = pl.ds(pair * 2 * lanes, 2 * lanes)
-            planes = near[:, at] + dot(far, gather[pl.ds(6 * lanes, 4 * lanes), at])
+            planes = near[:, at] + dot(far, gather[pl.ds(6 * lanes, lanes), at])
             use(2 * pair, planes[:, :lanes])
             use(2 * pair + 1, planes[:, lanes:])
 
@@ -589,6 +609,9 @@
         keep, gain = ratio_next * ratio, 2.0 * ratio_next / half_width
         ratio = ratio_next
         start_faces(now, sweep + 1)
+        if sweep > 1:
+            for f in range(6):
+                face_update(change, PAD, f, near[:, pl.ds(f * lanes, lanes)])
 
         def relax(n, carry, now=now, then=then, keep=keep, gain=gain, sweep=sweep):
             here = now[at_chunk(n), :]
@@ -605,7 +628,7 @@
             added = gain * face_link[f] * planes
             face_update(then, PAD, f, added)
             if sweep < SWEEPS - 1:
-                face_update(change, PAD, f, added)
+                near[:, pl.ds(f * lanes, lanes)] = added
 
         finish_faces(sweep + 1, add_faces)
         now, then = then, now
@@ -614,7 +637,7 @@
         out_ref[:, pl.ds(pl.multiple_of(t * PLANE, PLANE), PLANE)] = now[rows_of(t), :].T
         return carry
 
-    lax.fori_loop(0, B, write_out, 0, unroll=2)
+    lax.fori_loop(0, B, write_out, 0, unroll=4)
 
     for round_ in range(SWEEPS + 1):
         for copy in face_copies(round_):
@@ -660,14 +683,14 @@
             tall_field,
             tall_field,
             tall_field,
-            pltpu.VMEM((10 * lanes, 6 * lanes), BF16),
+            pltpu.VMEM((7 * lanes, 6 * lanes), BF16),
             pltpu.VMEM((6 * lanes, lanes), BF16),
             pltpu.VMEM((6, PLANE, lanes), F32),
             pltpu.VMEM((PLANE, lanes), F32),
             pltpu.VMEM((2, PLANE, 6 * lanes), BF16),
             pltpu.VMEM((PLANE, 6 * lanes), BF16),
-            pltpu.VMEM((SWEEPS + 1, PLANE, lanes), BF16),
-            pltpu.VMEM((SWEEPS + 1, 4, PLANE, lanes), BF16),
+            pltpu.VMEM((SWEEPS + 1, 4, FOLD, lanes), BF16),
+            pltpu.VMEM((SWEEPS + 1, 4, FOLD, lanes), BF16),
             pltpu.VMEM((6, PLANE, lanes), F32),
             pltpu.VMEM((PLANE, 6 * lanes), F32),
             pltpu.SemaphoreType.DMA((3,)),

time: 102 us -> 101 us (level)
    pallas_call x1, Pallas kernels: 100 us -> 99.4 us  [local(): pl.pallas_call(functools.partial(kernel, devices, minor), out_shape=pltpu...]
where the time goes in v3:
time: 101 us
  Pallas kernels  99.4 us (98%)
  local copies, waits for them, and re-layouts  1.32 us (1%)
    pallas_call x1, Pallas kernels, local(): pl.pallas_call(functools.partial(kernel, devices, minor), out_shape=pltpu...  99.4 us

profile of v3, /device:TPU:1, one launch (start us, length us, event | category | flops | bytes accessed | tf_op | source)
XLA Modules:
  0.0 100.7 jit_solution(12793515944514339078)
XLA Ops:
  0.0 99.4 %shard_map.82 = f32[128,4096]{1,0:T(8,128)S(1)} custom-call(s32[1,256]{1,0:T(1,128)} %bitcast.2, s32[1,128]{1,0:T(1,128)} %bitcast.3, s32[6,128]{1,0:T(8,128)} %tile_ref.1, s32[6,128]{1,0:T(8,128)} %side_ref.1, s32[6,128]{1,0:T(8,128)} %turn_ref.1, f32[256,4096]{1,0:T(8,128)} %warm_hbm.1, bf16[256,4096]{1,0:T(8,128)(2,1)} %heat_hbm.1, ...), custom_call_target="tpu_custom_call" | custom-call | tf_op jit(solution)/shard_map/pallas_call | solution.py:660
  99.4 1.3 %copy.10 = f32[128,4096]{1,0:T(8,128)} copy(f32[128,4096]{1,0:T(8,128)S(1)} %shard_map.82) | data formatting | bytes 4194304

commit v4 on v3

--- a/solution.py
+++ b/solution.py
@@ -132,7 +132,7 @@
     barrier = pltpu.get_barrier_semaphore()
 
     def peer(t):
-        p = lax.rem(me + t * 37, devices)
+        p = lax.rem(me + t * 85, devices)
         return p, (lax.div(p, minor), lax.rem(p, minor))
 
     def greet(t, carry):

time: 101 us -> 98.1 us (0.971)
  Pallas kernels: 99.4 us -> 96 us
    pallas_call x1, Pallas kernels: 99.4 us -> 96 us  [local(): pl.pallas_call(functools.partial(kernel, devices, minor), out_shape=pltpu...]
where the time goes in v4:
time: 98.1 us; the launch traced here: 97.3 us
  Pallas kernels  96 us (98%)
  local copies, waits for them, and re-layouts  1.32 us (1%)
    pallas_call x1, Pallas kernels, local(): pl.pallas_call(functools.partial(kernel, devices, minor), out_shape=pltpu...  96 us

profile of v4, /device:TPU:1, one launch (start us, length us, event | category | flops | bytes accessed | tf_op | source)
XLA Modules:
  0.0 97.3 jit_solution(3568986389987528819)
XLA Ops:
  0.0 96.0 %shard_map.82 = f32[128,4096]{1,0:T(8,128)S(1)} custom-call(s32[1,256]{1,0:T(1,128)} %bitcast.2, s32[1,128]{1,0:T(1,128)} %bitcast.3, s32[6,128]{1,0:T(8,128)} %tile_ref.1, s32[6,128]{1,0:T(8,128)} %side_ref.1, s32[6,128]{1,0:T(8,128)} %turn_ref.1, f32[256,4096]{1,0:T(8,128)} %warm_hbm.1, bf16[256,4096]{1,0:T(8,128)(2,1)} %heat_hbm.1, ...), custom_call_target="tpu_custom_call" | custom-call | tf_op jit(solution)/shard_map/pallas_call | solution.py:660
  96.0 1.3 %copy.10 = f32[128,4096]{1,0:T(8,128)} copy(f32[128,4096]{1,0:T(8,128)S(1)} %shard_map.82) | data formatting | bytes 4194304
